TPU v7x, 32 devices: a whole 2x2x4 slice. The times are simulated.
32 devices in a mesh: groups: 2 (over y), replica: 4 (over z), tensor: 4 (over x, core).
Axes of the slice: x: 2, y: 2, z: 4, core: 2. Of those that a mesh axis runs over, the one named last changes fastest.
Arguments:
- queries: bfloat16 [2, 256, 4, 512], P(None, ('groups', 'replica'), 'tensor'), parts along dimension 1, may hold values from -130 to 130
- key_cache: bfloat16 [256, 4, 16, 128], P(('groups', 'replica'), 'tensor'), parts along dimension 0, may hold values from -6 to 6
- value_cache: bfloat16 [256, 4, 16, 128], P(('groups', 'replica'), 'tensor'), parts along dimension 0, may hold values from -6 to 6
- decoded_keys: bfloat16 [2, 256, 4, 128], P(None, ('groups', 'replica'), 'tensor'), parts along dimension 1, may hold values from -6 to 6
- decoded_values: bfloat16 [2, 256, 4, 128], P(None, ('groups', 'replica'), 'tensor'), parts along dimension 1, may hold values from -6 to 6
- lengths: int32 [256], P(('groups', 'replica')), parts along dimension 0, may hold values from 1 to 16, 1024 in all
- request_adapters: int32 [256], P(('groups', 'replica')), parts along dimension 0, may hold values from 0 to 31, as said below
- table_row_of: int32 [64], P('groups'), parts along dimension 0, may hold values from 0 to 31, as said below
- output_matrix: bfloat16 [2048, 4096], P('tensor'), may hold values from -0.125 to 0.125
- down_maps: bfloat16 [32, 4, 512, 16], P('replica', 'tensor'), may hold values from -0.125 to 0.125
- up_maps: bfloat16 [32, 16, 4096], P('replica', None, 'tensor'), may hold values from -1.5 to 1.5
Outputs:
- projected: bfloat16 [2, 256, 4096], P(None, ('groups', 'replica'), 'tensor'), parts along dimension 1
There are 2 independent parts, one for each index of `groups`. A program takes and returns all parts, laid end to end along the dimension named above; an argument that names none is the same for every part. Nothing has to cross between parts.
Inputs may be any that keep to these rules, and one draw needn't show every extreme that they name: table_row_of is a permutation; adapter a lies with replica table_row_of[a] // 8. `request_adapters`: among the 32 requests of one replica (aligned blocks), at most 16 name adapters that lie with the same replica, and in every block some replica is named exactly 16 times.
All inputs are finite; a program needn't handle non-finite values. No bound on the sum of `lengths` on one device may be relied on, other than what follows from the above.
Results may differ from a plain program's by a relative error of at most 0.008.
Values may be sent and summed in bfloat16 or wider, within the bound.
A program may use at most 64 MiB of HBM per device.

v0:
```python
import math

import jax
import jax.numpy as jnp
from jax import lax
from jax.sharding import PartitionSpec as P

ADAPTER_SCALE = 2.0


def attend(queries, key_cache, value_cache, decoded_keys, decoded_values, lengths):
    steps, rows, groups, feature_width = queries.shape
    head = key_cache.shape[-1]
    cache_len = key_cache.shape[2]
    per_group = feature_width // head
    scale = 1.0 / math.sqrt(head)
    query = queries.reshape(steps, rows, groups, per_group, head)
    cached = (
        jnp.einsum("srgjd,rgpd->srgjp", query, key_cache, preferred_element_type=jnp.float32)
        * scale
    )
    valid = jnp.arange(cache_len, dtype=jnp.int32)[None, :] < lengths[:, None]
    cached = jnp.where(valid[None, :, None, None, :], cached, -jnp.inf)
    fresh = (
        jnp.einsum("srgjd,trgd->srgjt", query, decoded_keys, preferred_element_type=jnp.float32)
        * scale
    )
    causal = (
        jnp.arange(steps, dtype=jnp.int32)[None, :] <= jnp.arange(steps, dtype=jnp.int32)[:, None]
    )
    fresh = jnp.where(causal[:, None, None, None, :], fresh, -jnp.inf)
    top = jnp.maximum(jnp.max(cached, axis=-1), jnp.max(fresh, axis=-1))
    exp_cached = jnp.exp(cached - top[..., None])
    exp_fresh = jnp.exp(fresh - top[..., None])
    total = jnp.sum(exp_cached, axis=-1) + jnp.sum(exp_fresh, axis=-1)
    weight_cached = (exp_cached / total[..., None]).astype(jnp.bfloat16)
    weight_fresh = (exp_fresh / total[..., None]).astype(jnp.bfloat16)
    mixed = jnp.einsum(
        "srgjp,rgpd->srgjd", weight_cached, value_cache, preferred_element_type=jnp.float32
    )
    mixed = mixed + jnp.einsum(
        "srgjt,trgd->srgjd", weight_fresh, decoded_values, preferred_element_type=jnp.float32
    )
    return mixed.astype(jnp.bfloat16).reshape(steps, rows, groups * feature_width)


def per_device(
    queries,
    key_cache,
    value_cache,
    decoded_keys,
    decoded_values,
    lengths,
    request_adapters,
    table_row_of,
    output_matrix,
    down_maps,
    up_maps,
):
    steps, rows = (queries.shape[0], queries.shape[1])
    heads = attend(queries, key_cache, value_cache, decoded_keys, decoded_values, lengths)
    feature_width = heads.shape[-1]
    partial_base = jnp.dot(
        heads.reshape(steps * rows, feature_width),
        output_matrix,
        preferred_element_type=jnp.float32,
    )
    base = lax.psum_scatter(partial_base, "tensor", scatter_dimension=1, tiled=True)
    output_columns = base.shape[-1]
    base = base.reshape(steps, rows, output_columns)
    owner_count = lax.axis_size("replica")
    owner_share = down_maps.shape[0]
    capacity = max(2, 2 * rows // owner_count)
    stored = table_row_of[request_adapters]
    owner = stored // owner_share
    local = stored % owner_share
    same = owner[:, None] == owner[None, :]
    earlier = (
        jnp.arange(rows, dtype=jnp.int32)[None, :] < jnp.arange(rows, dtype=jnp.int32)[:, None]
    )
    rank_in = jnp.sum(jnp.where(same & earlier, 1, 0), axis=1).astype(jnp.int32)
    slot = owner * capacity + rank_in
    onehot = slot[:, None] == jnp.arange(owner_count * capacity, dtype=jnp.int32)[None, :]
    requests = jnp.sum(jnp.where(onehot, local[:, None], 0), axis=0).reshape(owner_count, capacity)
    rank_width = up_maps.shape[1]
    placed = jnp.einsum(
        "rn,srh->nsh", onehot.astype(jnp.bfloat16), heads, preferred_element_type=jnp.float32
    )
    placed = placed.astype(jnp.bfloat16).reshape(owner_count, capacity, steps * feature_width)
    sent_heads = lax.all_to_all(placed, "replica", split_axis=0, concat_axis=0, tiled=True)
    needed_adapters = lax.all_to_all(requests, "replica", split_axis=0, concat_axis=0, tiled=True)
    tally_count = needed_adapters.shape[1]
    down_rows = down_maps[needed_adapters].reshape(
        owner_count, tally_count, feature_width, rank_width
    )
    low_part = jnp.einsum(
        "nksh,nkhr->nksr",
        sent_heads.reshape(owner_count, tally_count, steps, feature_width),
        down_rows,
        preferred_element_type=jnp.float32,
    )
    lower_product = lax.psum(low_part, "tensor")
    up_rows = up_maps[needed_adapters].astype(jnp.float32)
    result = (
        ADAPTER_SCALE
        * jnp.einsum("nksr,nkro->nkso", lower_product, up_rows, precision=lax.Precision.HIGHEST)
    ).astype(jnp.bfloat16)
    returned = lax.all_to_all(
        result.reshape(owner_count, tally_count, steps * output_columns),
        "replica",
        split_axis=0,
        concat_axis=0,
        tiled=True,
    )
    returned = returned.reshape(owner_count * capacity, steps, output_columns)
    delta = jnp.einsum(
        "rn,nso->sro", onehot.astype(jnp.bfloat16), returned, preferred_element_type=jnp.float32
    ).astype(jnp.bfloat16)
    return (base + delta.astype(jnp.float32)).astype(jnp.bfloat16)


def solution(mesh):
    return jax.shard_map(
        per_device,
        mesh=mesh,
        in_specs=(
            P(None, ("groups", "replica"), "tensor", None),
            P(("groups", "replica"), "tensor", None, None),
            P(("groups", "replica"), "tensor", None, None),
            P(None, ("groups", "replica"), "tensor", None),
            P(None, ("groups", "replica"), "tensor", None),
            P(("groups", "replica")),
            P(("groups", "replica")),
            P("groups"),
            P("tensor", None),
            P("replica", "tensor", None, None),
            P("replica", None, "tensor"),
        ),
        out_specs=P(None, ("groups", "replica"), "tensor"),
        check_vma=False,
    )
```

profile of v0, /device:TPU:0, one launch (start us, length us, event | category | flops | bytes accessed | tf_op | source)
XLA Modules:
  0.0 74.0 jit_solution(11879619882770487263)
XLA Ops:
  6.5 0.0 copy-start
  6.5 0.0 copy-start.4
  6.5 0.0 reduce-scatter.2.cloned.1.call-start
  6.5 0.9 %reshape.207 = bf16[2,32,4,128]{3,2,1,0:T(4,128)(2,1)S(1)} reshape(bf16[2,32,1,512]{3,1,2,0:T(8,128)(2,1)} %param.11) | data formatting | bytes 131072 | tf_op jit(solution)/shard_map/reshape.2
  7.5 0.7 iota_compare_fusion.2
  8.2 1.2 %fusion.36 = (f32[2,32,4]{2,0,1:T(2,128)S(1)}, f32[2,32,1,4,16]{4,3,0,1,2:T(4,128)S(1)}) fusion(bf16[2,32,4,128]{3,2,1,0:T(4,128)(2,1)S(1)} %reshape.207, bf16[32,1,16,128]{3,2,1,0:T(8,128)(2,1)} %param.12, pred[32,16]{1,0:T(8,128)(4,1)S(1)} %iota_compare_fusion.2), kind=kOutput, calls=%fused_computation.63 | convolution fusion | flops 1060608 | bytes 214528 | tf_op jit(solution)/shard_map/srgjd,rgpd->srgjp/dot_general | solution.py:19
  9.4 1.4 %fusion.37 = (f32[2,32,4]{2,0,1:T(2,128)S(1)}, f32[2,32,1,4,2]{3,4,0,1,2:T(2,128)S(1)}) fusion(bf16[2,32,4,128]{3,2,1,0:T(4,128)(2,1)S(1)} %reshape.207, bf16[2,32,128,1]{2,1,0,3:T(8,128)(2,1)} %bitcast.87, pred[2,2]{1,0:T(4,128)(4,1)S(1)} %iota_compare_fusion.3), kind=kOutput, calls=%fused_computation.64 | convolution fusion | flops 132352 | bytes 84996 | tf_op jit(solution)/shard_map/srgjd,trgd->srgjt/dot_general | solution.py:25
  10.9 0.1 fusion.24
  11.0 0.3 fusion.15
  11.3 0.0 copy-start.3
  11.3 1.1 %fusion.25 = f32[32,2,4,128]{3,2,1,0:T(4,128)S(1)} fusion(f32[2,32,1,4,2]{3,4,0,1,2:T(2,128)S(1)} %get-tuple-element.10, f32[2,32,4]{2,0,1:T(2,128)S(1)} %add.68, f32[2,32,4]{2,0,1:T(2,128)S(1)} %max.9, bf16[2,32,128,1]{2,1,0,3:T(8,128)(2,1)} %bitcast.88), kind=kOutput, calls=%fused_computation.38 | convolution fusion | flops 132608 | bytes 151552 | tf_op jit(solution)/shard_map/srgjt,trgd->srgjd/dot_general | solution.py:41
  12.5 0.0 copy-done.4
  12.5 0.4 fusion.7
  12.9 0.7 copy-done.3
  13.5 0.0 copy-start.5
  13.5 0.0 copy-start.2
  13.5 1.8 %fusion.16 = f32[64,4096]{1,0:T(8,128)} fusion(bf16[512,4096]{1,0:T(8,128)(2,1)S(1)} %copy-done.3, bf16[8,8,4,128]{3,2,1,0:T(4,128)(2,1)S(1)} %bitcast.85), kind=kOutput, calls=%fused_computation.27 | convolution fusion | flops 268435456 | bytes 5308416 | tf_op jit(solution)/shard_map/dot_general | solution.py:63
  15.4 0.0 copy-start.1
  15.4 0.0 reduce-scatter.2.cloned.1.call-update
  15.4 0.0 copy-done.5
  15.4 0.0 copy-done.2
  15.4 0.7 gather_fusion
  16.2 0.2 select_reduce_fusion.1
  16.3 0.1 select_reduce_fusion
  16.4 0.7 all_to_all.15
  17.1 6.3 %all-to-all-start.1 = ((s32[4,1,16]{2,1,0:T(1,128)}), s32[4,1,16]{2,1,0:T(1,128)S(1)}, u32[]{:S(2)}, u32[]{:S(2)}) async-start(s32[4,1,16]{2,1,0:T(1,128)} %bitcast.24), calls=%async_computation.2 | async-start | bytes 4096 | tf_op jit(solution)/shard_map/all_to_all | solution.py:91
  23.5 0.3 convolution_convert_fusion.1
  23.8 0.1 copy.40
  23.9 0.7 reshape.215
  24.6 4.2 %all-to-all-done.1 = s32[4,1,16]{2,1,0:T(1,128)S(1)} async-done(((s32[4,1,16]{2,1,0:T(1,128)}), s32[4,1,16]{2,1,0:T(1,128)S(1)}, u32[]{:S(2)}, u32[]{:S(2)}) %all-to-all-start.1) | async-done | bytes 288 | tf_op jit(solution)/shard_map/all_to_all | solution.py:91
  28.8 3.9 %all-to-all-start = ((bf16[4,16,1024]{2,1,0:T(8,128)(2,1)}), bf16[4,16,1024]{2,1,0:T(8,128)(2,1)}, u32[]{:S(2)}, u32[]{:S(2)}) async-start(bf16[4,16,1024]{2,1,0:T(8,128)(2,1)} %reshape.215), calls=%async_computation.1 | async-start | bytes 262144 | tf_op jit(solution)/shard_map/all_to_all | solution.py:90
  32.8 0.1 reshape.232
  32.9 0.0 copy-done.1
  32.9 0.6 gather_fusion.1
  33.5 0.0 copy-done
  33.5 0.7 gather_fusion.2
  34.2 4.6 %all-to-all-done = bf16[4,16,1024]{2,1,0:T(8,128)(2,1)} async-done(((bf16[4,16,1024]{2,1,0:T(8,128)(2,1)}), bf16[4,16,1024]{2,1,0:T(8,128)(2,1)}, u32[]{:S(2)}, u32[]{:S(2)}) %all-to-all-start) | async-done | bytes 131104 | tf_op jit(solution)/shard_map/all_to_all | solution.py:90
  38.7 1.0 %reshape.216 = bf16[4,16,2,512]{3,2,1,0:T(2,128)(2,1)S(1)} reshape(bf16[4,16,1024]{2,1,0:T(8,128)(2,1)} %all-to-all-done) | data formatting | bytes 262144 | tf_op jit(solution)/shard_map/reshape | solution.py:98
  39.7 1.1 %fusion.38 = f32[4,16,2,16]{3,2,1,0:T(2,128)} fusion(bf16[4,16,2,512]{3,2,1,0:T(2,128)(2,1)S(1)} %reshape.216, bf16[4,16,512,16]{2,3,1,0:T(8,128)(2,1)S(1)} %bitcast.82), kind=kOutput, calls=%fused_computation.65 | convolution fusion | flops 2097152 | bytes 1187840 | tf_op jit(solution)/shard_map/nksh,nkhr->nksr/dot_general | solution.py:96
  40.8 11.2 %psum.7 = f32[4,16,2,16]{3,2,1,0:T(2,128)S(1)} all-reduce(f32[4,16,2,16]{3,2,1,0:T(2,128)} %fusion.38), channel_id=1, replica_groups=mesh['groups'=2,'replica'=4,'tensor'=4] {'tensor'}, use_global_device_ids=true, to_apply=%region_7.8 | all-reduce | flops 2048 | bytes 16384 | tf_op jit(solution)/shard_map/psum | solution.py:102
  52.0 1.0 %fusion = bf16[4,16,2,1024]{3,2,1,0:T(2,128)(2,1)S(1)} fusion(f32[4,16,2,16]{3,2,1,0:T(2,128)S(1)} %psum.7, bf16[4,16,16,1024]{3,2,1,0:T(8,128)(2,1)S(1)} %bitcast.83), kind=kOutput, calls=%fused_computation.4 | convolution fusion | flops 25427968 | bytes 2367488 | tf_op jit(solution)/shard_map/nksr,nkro->nkso/dot_general | solution.py:106
  53.0 0.2 reshape.218
  53.2 11.9 %all_to_all.22 = bf16[4,16,2048]{2,1,0:T(8,128)(2,1)S(1)} all-to-all(bf16[4,16,2048]{2,1,0:T(8,128)(2,1)S(1)} %reshape.218), channel_id=1, replica_groups=mesh['groups'=2,'replica'=4,'tensor'=4] {'replica'}, dimensions={0} | all-to-all | bytes 524288 | tf_op jit(solution)/shard_map/all_to_all | solution.py:108
  65.1 0.2 reshape.219
  65.3 0.0 reduce-scatter.2.cloned.1.call-done
  65.3 1.8 %fusion.4 = bf16[2,32,1024]{2,1,0:T(8,128)(2,1)} fusion(f32[2,32,1024]{2,1,0:T(8,128)} %bitcast.84, bf16[64,2,1024]{2,1,0:T(2,128)(2,1)S(1)} %reshape.219, s32[32]{0:T(128)S(1)} %multiply_add_fusion), kind=kOutput, calls=%fused_computation.9 | convolution fusion | flops 8652800 | bytes 655488 | tf_op jit(solution)/shard_map/rn,nso->sro/dot_general | solution.py:116
  (11 shorter events, 0.1 us)
Async XLA Ops:
  6.5 27.0 %copy-start = (bf16[8,16,1024]{2,1,0:T(8,128)(2,1)S(1)}, bf16[8,16,1024]{2,1,0:T(8,128)(2,1)}, u32[]{:S(2)}) copy-start(bf16[8,16,1024]{2,1,0:T(8,128)(2,1)} %param.21) | copy-start | bytes 786436
  6.5 5.9 %copy-start.4 = (bf16[32,1,16,128]{3,2,1,0:T(8,128)(2,1)S(1)}, bf16[32,1,16,128]{3,2,1,0:T(8,128)(2,1)}, u32[]{:S(2)}) copy-start(bf16[32,1,16,128]{3,2,1,0:T(8,128)(2,1)} %param.13) | copy-start | bytes 393220
  6.5 58.8 %reduce-scatter.2.cloned.1.call-start = ((), (), s32[]{:S(2)}) async-start(), calls=%async_computation.4 | async-start | bytes 1310720 | tf_op jit(solution)/shard_map/reduce_scatter | solution.py:68
  11.3 2.2 %copy-start.3 = (bf16[512,4096]{1,0:T(8,128)(2,1)S(1)}, bf16[512,4096]{1,0:T(8,128)(2,1)}, u32[]{:S(2)}) copy-start(bf16[512,4096]{1,0:T(8,128)(2,1)} %param.19) | copy-start | bytes 12582916
  13.5 1.9 %copy-start.5 = (s32[32]{0:T(128)S(1)}, s32[32]{0:T(128)}, u32[]{:S(2)}) copy-start(s32[32]{0:T(128)} %param.17) | copy-start | bytes 388
  13.5 1.9 %copy-start.2 = (s32[32]{0:T(128)S(1)}, s32[32]{0:T(128)}, u32[]{:S(2)}) copy-start(s32[32]{0:T(128)} %param.18) | copy-start | bytes 388
  15.4 17.5 %copy-start.1 = (bf16[8,1,512,16]{2,3,1,0:T(8,128)(2,1)S(1)}, bf16[8,1,512,16]{2,3,1,0:T(8,128)(2,1)}, u32[]{:S(2)}) copy-start(bf16[8,1,512,16]{2,3,1,0:T(8,128)(2,1)} %param.20) | copy-start | bytes 393220
  17.1 11.7 %all-to-all-start.1 = ((s32[4,1,16]{2,1,0:T(1,128)}), s32[4,1,16]{2,1,0:T(1,128)S(1)}, u32[]{:S(2)}, u32[]{:S(2)}) async-start(s32[4,1,16]{2,1,0:T(1,128)} %bitcast.24), calls=%async_computation.2 | async-start | bytes 4096 | tf_op jit(solution)/shard_map/all_to_all | solution.py:91
  28.8 9.9 %all-to-all-start = ((bf16[4,16,1024]{2,1,0:T(8,128)(2,1)}), bf16[4,16,1024]{2,1,0:T(8,128)(2,1)}, u32[]{:S(2)}, u32[]{:S(2)}) async-start(bf16[4,16,1024]{2,1,0:T(8,128)(2,1)} %reshape.215), calls=%async_computation.1 | async-start | bytes 262144 | tf_op jit(solution)/shard_map/all_to_all | solution.py:90
Sparse Core Ops, SparseCore 0:
  15.5 27.5 reduce-scatter.1
where the time goes:
time: 74.6 us; the launch traced here: 74 us
  blocking collectives  23.1 us (31%)
  between operations  13.6 us (18%)
  starting transfers between devices  10.3 us (14%)
  matrix products  10.2 us (14%)
  waiting for transfers between devices  8.78 us (12%)
  local copies, waits for them, and re-layouts  6.64 us (9%)
  other arithmetic  1.5 us (2%)
    all_to_all x1, blocking collectives, per_device(): lax.all_to_all(result.reshape(owner_count, tally_count, steps * output_co...  11.9 us
    psum x1, blocking collectives, per_device(): lower_product = lax.psum(low_part, 'tensor')  11.2 us
    all_to_all x1, starting transfers between devices, per_device(): lax.all_to_all(requests, 'replica', split_axis=0, concat_axis=0, tiled=True)  6.32 us
    all_to_all x1, waiting for transfers between devices, per_device(): lax.all_to_all(placed, 'replica', split_axis=0, concat_axis=0, tiled=True)  4.55 us
    all_to_all x1, waiting for transfers between devices, per_device(): lax.all_to_all(requests, 'replica', split_axis=0, concat_axis=0, tiled=True)  4.19 us
    all_to_all x1, starting transfers between devices, per_device(): lax.all_to_all(placed, 'replica', split_axis=0, concat_axis=0, tiled=True)  3.94 us
    dot_general x1, matrix products, per_device(): jnp.einsum('rn,nso->sro', onehot.astype(jnp.bfloat16), returned, preferre...  1.84 us
    dot_general x1, matrix products, per_device(): jnp.dot(heads.reshape(steps * rows, feature_width), output_matrix, prefer...  1.83 us
  transfers between devices with their start and end apart: 3, of which 2 were waited for; matrix products, arithmetic and copies ran while one was open for 9% of the time, Pallas kernels for 0%

commit v1 on v0

v1 whole, which is shorter than its diff:
```python
import functools
import math

import jax
import jax.numpy as jnp
from jax import lax
from jax.experimental import pallas as pl
from jax.experimental.pallas import tpu as pltpu
from jax.sharding import PartitionSpec as P

ADAPTER_SCALE = 2.0
MASKED = -1e30
MESH = pl.DeviceIdType.MESH
F32 = jnp.float32
BF16 = jnp.bfloat16


def iota(shape, dim):
    return lax.broadcasted_iota(jnp.int32, shape, dim)


def dot(a, b):
    return jnp.dot(a, b, preferred_element_type=F32)


def dot_t(a, b):
    return lax.dot_general(a, b, (((1,), (1,)), ((), ())), preferred_element_type=F32)


def aligned(start, size):
    return pl.ds(pl.multiple_of(start * size, size), size)


def to_column(row):
    n = row.shape[1]
    eye = iota((n, n), 0) == iota((n, n), 1)
    return jnp.sum(jnp.where(eye, row, 0.0), axis=1, keepdims=True)


def to_row(column):
    n = column.shape[0]
    eye = iota((n, n), 0) == iota((n, n), 1)
    return jnp.sum(jnp.where(eye, column, 0.0), axis=0, keepdims=True)


def each(count, body):
    if count <= 8:
        for i in range(count):
            body(i)
    else:
        lax.fori_loop(0, count, lambda i, c: (body(i), c)[1], 0)


def kernel(
    dims,
    lengths_ref,
    adapters_ref,
    table_ref,
    query_hbm,
    key_hbm,
    value_hbm,
    new_key_hbm,
    new_value_hbm,
    matrix_hbm,
    down_hbm,
    up_hbm,
    out_ref,
    query,
    keys,
    values,
    matrix,
    down,
    up,
    heads,
    heads_out,
    heads_in,
    mask_out,
    mask_in,
    low_out,
    low_in,
    delta_out,
    delta_in,
    base_own,
    base_out,
    base_in,
    local_sem,
    mask_send,
    mask_recv,
    heads_send,
    heads_recv,
    low_send,
    low_recv,
    delta_send,
    delta_recv,
    base_send,
    base_recv,
):
    steps, rows, cache, head, owners, tensors, share, rank, cap, chunk = dims
    me = lax.axis_index("replica")
    mine = lax.axis_index("tensor")
    columns = out_ref.shape[1]
    cached = rows * cache
    per_group = query.shape[1] // head

    def ring(off):
        return lax.rem(me + off, owners)

    def back(off):
        return lax.rem(me + owners - off, owners)

    def peer(k):
        if tensors % 2:
            return lax.rem(mine + k, tensors)
        flipped = mine // 2 * 2 + (mine % 2 + k % 2) % 2
        return (flipped + k // 2 * 2) % tensors

    barrier = pltpu.get_barrier_semaphore()

    def greet(i):
        pl.semaphore_signal(
            barrier, inc=1, device_id={"replica": ring(i + 1)}, device_id_type=MESH
        )

    each(owners - 1, greet)
    for k in range(1, tensors):
        pl.semaphore_signal(barrier, inc=1, device_id={"tensor": peer(k)}, device_id_type=MESH)

    loads = [
        (query_hbm, query),
        (key_hbm, keys.at[pl.ds(0, cached)]),
        (new_key_hbm, keys.at[pl.ds(cached, steps * rows)]),
        (value_hbm, values.at[pl.ds(0, cached)]),
        (new_value_hbm, values.at[pl.ds(cached, steps * rows)]),
        (down_hbm, down),
        (matrix_hbm, matrix),
        (up_hbm, up),
    ]
    loads = [pltpu.make_async_copy(a, b, local_sem.at[i]) for i, (a, b) in enumerate(loads)]
    for load in loads:
        load.start()

    wanted = to_column(adapters_ref[...].astype(F32))
    total = table_ref.shape[1]
    hit = wanted == iota((rows, total), 1).astype(F32)
    stored = jnp.sum(jnp.where(hit, table_ref[...].astype(F32), 0.0), axis=1, keepdims=True)
    owner = jnp.floor((stored + 0.5) / share)
    local = stored - owner * share
    owner_row = to_row(owner)
    earlier = iota((rows, rows), 1) < iota((rows, rows), 0)
    rank_in = jnp.sum(
        jnp.where(earlier & (owner == owner_row), 1.0, 0.0), axis=1, keepdims=True
    )
    slot = owner * chunk + rank_in
    slot_row = to_row(slot)
    places = owners * chunk
    place_row = iota((places, rows), 0).astype(F32)
    place_col = iota((rows, places), 1).astype(F32)
    pick = [
        jnp.where(place_row == slot_row + s * cap, 1.0, 0.0).astype(BF16) for s in range(steps)
    ]
    unpick = [
        jnp.where(place_col == slot + s * cap, 1.0, 0.0).astype(BF16) for s in range(steps)
    ]
    unpick = jnp.concatenate(unpick, axis=0)
    width = share * rank
    low_column = iota((rows, width), 1).astype(F32)
    of_local = (low_column >= local * rank) & (low_column < (local + 1.0) * rank)
    of_local = jnp.where(of_local, 1.0, 0.0).astype(BF16)
    mask_out[...] = sum(dot(p, of_local) for p in pick).astype(BF16)

    pl.semaphore_wait(barrier, owners + tensors - 2)

    def exchange(out, into, send, recv, dest):
        return pltpu.make_async_remote_copy(
            src_ref=out.at[aligned(dest, chunk)],
            dst_ref=into.at[aligned(me, chunk)],
            send_sem=send.at[dest],
            recv_sem=recv.at[me],
            device_id={"replica": dest},
            device_id_type=MESH,
        )

    def arrival(out, into, send, recv, source):
        return pltpu.make_async_remote_copy(
            src_ref=out.at[aligned(source, chunk)],
            dst_ref=into.at[aligned(source, chunk)],
            send_sem=send.at[source],
            recv_sem=recv.at[source],
            device_id={"replica": source},
            device_id_type=MESH,
        )

    masks = (mask_out, mask_in, mask_send, mask_recv)
    placed = (heads_out, heads_in, heads_send, heads_recv)
    deltas = (delta_out, delta_in, delta_send, delta_recv)
    each(owners - 1, lambda i: exchange(*masks, ring(i + 1)).start())

    length = to_column(lengths_ref[...].astype(F32))
    every = cached + steps * rows
    place = iota((rows, every), 1).astype(F32)
    request = iota((rows, 1), 0).astype(F32)
    first = request * cache
    visible = (place >= first) & (place < first + length)
    allowed = []
    for s in range(steps):
        visible = visible | (place == request + (cached + s * rows))
        allowed.append(jnp.where(visible, 0.0, MASKED))
    bias = jnp.concatenate(allowed, axis=0)
    scale = 1.0 / math.sqrt(head)
    for load in loads[:5]:
        load.wait()
    for j in range(per_group):
        part = pl.ds(j * head, head)
        scores = dot_t(query[:, part], keys[...]) * scale
        scores = jnp.where(bias < 0.0, MASKED, scores)
        top = jnp.max(scores, axis=1, keepdims=True)
        weights = jnp.exp(scores - top)
        weights = (weights / jnp.sum(weights, axis=1, keepdims=True)).astype(BF16)
        heads[:, part] = dot(weights, values[...]).astype(BF16)

    mixed = heads[...]
    heads_out[...] = sum(
        dot(pick[s], mixed[s * rows : (s + 1) * rows]) for s in range(steps)
    ).astype(BF16)
    each(owners - 1, lambda i: exchange(*placed, ring(i + 1)).start())

    def low_copy(part, k):
        return pltpu.make_async_remote_copy(
            src_ref=low_out.at[part],
            dst_ref=low_in.at[mine, part],
            send_sem=low_send.at[part, peer(k)],
            recv_sem=low_recv.at[part, mine],
            device_id={"tensor": peer(k)},
            device_id_type=MESH,
        )

    def low_arrival(part, k):
        return pltpu.make_async_remote_copy(
            src_ref=low_out.at[part],
            dst_ref=low_in.at[peer(k), part],
            send_sem=low_send.at[part, peer(k)],
            recv_sem=low_recv.at[part, peer(k)],
            device_id={"tensor": peer(k)},
            device_id_type=MESH,
        )

    def lower(part, source_heads, source_mask):
        low = dot_t(source_heads[...], down[...]) * source_mask[...].astype(F32)
        low_out[part] = low.astype(BF16)
        for k in range(1, tensors):
            low_copy(part, k).start()

    loads[5].wait()
    own = aligned(me, chunk)
    lower(me, heads_out.at[own], mask_out.at[own])

    def base_copy(k):
        return pltpu.make_async_remote_copy(
            src_ref=base_out.at[k - 1],
            dst_ref=base_in.at[k - 1],
            send_sem=base_send.at[k - 1],
            recv_sem=base_recv.at[k - 1],
            device_id={"tensor": peer(k)},
            device_id_type=MESH,
        )

    loads[6].wait()
    for k in range(1, tensors):
        base_out[k - 1] = dot(mixed, matrix[:, aligned(peer(k), columns)]).astype(BF16)
        if k == 1:
            base_copy(k).start()
    base_own[...] = dot(mixed, matrix[:, aligned(mine, columns)])

    def lower_arrived(i):
        source = back(i + 1)
        here = aligned(source, chunk)
        arrival(*masks, source).wait_recv()
        arrival(*placed, source).wait_recv()
        lower(source, heads_in.at[here], mask_in.at[here])

    each(owners - 1, lower_arrived)
    for k in range(2, tensors):
        base_copy(k).start()

    def raise_back(part):
        low = low_out[part].astype(F32)
        for k in range(1, tensors):
            low_arrival(part, k).wait_recv()
            low = low + low_in[peer(k), part].astype(F32)
        return dot((ADAPTER_SCALE * low).astype(BF16), up[...]).astype(BF16)

    loads[7].wait()

    def raise_arrived(i):
        source = back(i + 1)
        delta_out[aligned(source, chunk)] = raise_back(source)
        exchange(*deltas, source).start()

    each(owners - 1, raise_arrived)
    delta_in[own] = raise_back(me)

    for k in range(1, tensors):
        base_copy(k).wait_recv()
        base_own[...] += base_in[k - 1].astype(F32)

    each(owners - 1, lambda i: arrival(*deltas, ring(i + 1)).wait_recv())
    delta = dot(unpick, delta_in[...])
    out_ref[...] = (base_own[...] + delta).astype(BF16)

    def sent(i):
        dest = ring(i + 1)
        exchange(*masks, dest).wait_send()
        exchange(*placed, dest).wait_send()
        exchange(*deltas, dest).wait_send()

    each(owners - 1, sent)

    def low_sent(part):
        for k in range(1, tensors):
            low_copy(part, k).wait_send()

    each(owners, low_sent)
    for k in range(1, tensors):
        base_copy(k).wait_send()


def per_device(
    owners,
    tensors,
    queries,
    key_cache,
    value_cache,
    decoded_keys,
    decoded_values,
    lengths,
    request_adapters,
    table_row_of,
    output_matrix,
    down_maps,
    up_maps,
):
    steps, rows, _, feature_width = queries.shape
    _, _, cache, head = key_cache.shape
    share, rank, columns = up_maps.shape
    cap = max(2, 2 * rows // owners)
    chunk = -(-max(16, steps * cap) // 16) * 16
    width = share * rank
    places = owners * chunk
    every = rows * cache + steps * rows
    down = jnp.swapaxes(down_maps.reshape(share, feature_width, rank), 1, 2)
    dma = pltpu.SemaphoreType.DMA
    vmem = pl.BlockSpec(memory_space=pltpu.VMEM)
    anywhere = pl.BlockSpec(memory_space=pl.ANY)
    dims = (steps, rows, cache, head, owners, tensors, share, rank, cap, chunk)
    out = pl.pallas_call(
        functools.partial(kernel, dims),
        name="decode_attention",
        out_shape=jax.ShapeDtypeStruct((steps * rows, columns), BF16),
        in_specs=[vmem] * 3 + [anywhere] * 8,
        out_specs=vmem,
        scratch_shapes=[
            pltpu.VMEM((steps * rows, feature_width), BF16),
            pltpu.VMEM((every, head), BF16),
            pltpu.VMEM((every, head), BF16),
            pltpu.VMEM(output_matrix.shape, BF16),
            pltpu.VMEM((width, feature_width), BF16),
            pltpu.VMEM((width, columns), BF16),
            pltpu.VMEM((steps * rows, feature_width), BF16),
            pltpu.VMEM((places, feature_width), BF16),
            pltpu.VMEM((places, feature_width), BF16),
            pltpu.VMEM((places, width), BF16),
            pltpu.VMEM((places, width), BF16),
            pltpu.VMEM((owners, chunk, width), BF16),
            pltpu.VMEM((tensors, owners, chunk, width), BF16),
            pltpu.VMEM((places, columns), BF16),
            pltpu.VMEM((places, columns), BF16),
            pltpu.VMEM((steps * rows, columns), F32),
            pltpu.VMEM((tensors - 1, steps * rows, columns), BF16),
            pltpu.VMEM((tensors - 1, steps * rows, columns), BF16),
            dma((8,)),
            dma((owners,)),
            dma((owners,)),
            dma((owners,)),
            dma((owners,)),
            dma((owners, tensors)),
            dma((owners, tensors)),
            dma((owners,)),
            dma((owners,)),
            dma((tensors - 1,)),
            dma((tensors - 1,)),
        ],
        compiler_params=pltpu.CompilerParams(
            collective_id=0, has_side_effects=True, vmem_limit_bytes=40 * 1024 * 1024
        ),
    )(
        lengths.reshape(1, rows),
        request_adapters.reshape(1, rows),
        table_row_of.reshape(1, -1),
        queries.reshape(steps * rows, feature_width),
        key_cache.reshape(rows * cache, head),
        value_cache.reshape(rows * cache, head),
        decoded_keys.reshape(steps * rows, head),
        decoded_values.reshape(steps * rows, head),
        output_matrix,
        down.reshape(width, feature_width),
        up_maps.reshape(width, columns),
    )
    return out.reshape(steps, rows, columns)


def solution(mesh):
    return jax.shard_map(
        functools.partial(per_device, mesh.shape["replica"], mesh.shape["tensor"]),
        mesh=mesh,
        in_specs=(
            P(None, ("groups", "replica"), "tensor", None),
            P(("groups", "replica"), "tensor", None, None),
            P(("groups", "replica"), "tensor", None, None),
            P(None, ("groups", "replica"), "tensor", None),
            P(None, ("groups", "replica"), "tensor", None),
            P(("groups", "replica")),
            P(("groups", "replica")),
            P("groups"),
            P("tensor", None),
            P("replica", "tensor", None, None),
            P("replica", None, "tensor"),
        ),
        out_specs=P(None, ("groups", "replica"), "tensor"),
        check_vma=False,
    )
```

time: 74.6 us -> 33.8 us (0.45)
  blocking collectives: 23.1 us -> 0 us
  Pallas kernels: 0 us -> 22.6 us
  between operations: 13.6 us -> 0.02 us
  starting transfers between devices: 10.3 us -> 0 us
  matrix products: 10.2 us -> 0 us
  waiting for transfers between devices: 8.78 us -> 0 us
  local copies, waits for them, and re-layouts: 6.64 us -> 10.7 us
  other arithmetic: 1.5 us -> 0 us
    pallas_call x0 -> x1, Pallas kernels: none -> 22.6 us  [per_device(): pl.pallas_call(functools.partial(kernel, dims), name='decode_attention',...]
    all_to_all x1 -> x0, blocking collectives: 11.9 us -> none  [per_device(): lax.all_to_all(result.reshape(owner_count, tally_count, steps * output_co...]
    psum x1 -> x0, blocking collectives: 11.2 us -> none  [per_device(): lower_product = lax.psum(low_part, 'tensor')]
    all_to_all x2 -> x0, starting transfers between devices: 10.3 us -> none  [the longest x1 6.32 us: per_device(): lax.all_to_all(requests, 'replica', split_axis=0, concat_axis=0, tiled=True)]
    dot_general x9 -> x0, matrix products: 10.2 us -> none  [the longest x1 1.84 us: per_device(): jnp.einsum('rn,nso->sro', onehot.astype(jnp.bfloat16), returned, preferre...]
    unnamed x12 -> x23, local copies, waits for them, and re-layouts: 0.69 us -> 10.7 us
    all_to_all x2 -> x0, waiting for transfers between devices: 8.74 us -> none  [the longest x1 4.55 us: per_device(): lax.all_to_all(placed, 'replica', split_axis=0, concat_axis=0, tiled=True)]
    reshape x5 -> x0, local copies, waits for them, and re-layouts: 2.11 us -> none  [the longest x1 0.99 us: per_device(): sent_heads.reshape(owner_count, tally_count, steps, feature_width)]
  transfers between devices with their start and end apart: 3 -> 0, of which waited for: 2 -> 0; matrix products, arithmetic and copies ran while one was open for 9% -> 0% of each run, Pallas kernels for 0% -> 0%
where the time goes in v1:
time: 33.8 us; the launch traced here: 33.3 us
  Pallas kernels  22.6 us (67%)
  local copies, waits for them, and re-layouts  10.7 us (32%)
    pallas_call x1, Pallas kernels, per_device(): pl.pallas_call(functools.partial(kernel, dims), name='decode_attention',...  22.6 us
    unnamed x23, local copies, waits for them, and re-layouts  10.7 us

profile of v1, /device:TPU:0, one launch (start us, length us, event | category | flops | bytes accessed | tf_op | source)
XLA Modules:
  0.0 33.3 jit_solution(8783308623020760296)
XLA Ops:
  0.0 0.0 copy-start
  0.0 2.2 %copy-done = bf16[512,4096]{1,0:T(8,128)(2,1)S(1)} copy-done((bf16[512,4096]{1,0:T(8,128)(2,1)S(1)}, bf16[512,4096]{1,0:T(8,128)(2,1)}, u32[]{:S(2)}) %copy-start) | copy-done | bytes 4194328
  2.2 0.0 copy-start.1
  2.2 0.9 %copy-done.1 = bf16[8,16,1024]{2,1,0:T(8,128)(2,1)S(1)} copy-done((bf16[8,16,1024]{2,1,0:T(8,128)(2,1)S(1)}, bf16[8,16,1024]{2,1,0:T(8,128)(2,1)}, u32[]{:S(2)}) %copy-start.1) | copy-done | bytes 262168
  3.1 0.0 copy-start.2
  3.1 0.9 %copy-done.2 = bf16[32,1,16,128]{3,2,1,0:T(8,128)(2,1)S(1)} copy-done((bf16[32,1,16,128]{3,2,1,0:T(8,128)(2,1)S(1)}, bf16[32,1,16,128]{3,2,1,0:T(8,128)(2,1)}, u32[]{:S(2)}) %copy-start.2) | copy-done | bytes 131096
  4.0 0.0 copy-start.3
  4.0 0.9 %copy-done.3 = bf16[32,1,16,128]{3,2,1,0:T(8,128)(2,1)S(1)} copy-done((bf16[32,1,16,128]{3,2,1,0:T(8,128)(2,1)S(1)}, bf16[32,1,16,128]{3,2,1,0:T(8,128)(2,1)}, u32[]{:S(2)}) %copy-start.3) | copy-done | bytes 131096
  4.9 0.0 copy-start.4
  5.0 0.9 %copy-done.4 = bf16[8,1,512,16]{2,3,1,0:T(8,128)(2,1)S(1)} copy-done((bf16[8,1,512,16]{2,3,1,0:T(8,128)(2,1)S(1)}, bf16[8,1,512,16]{2,3,1,0:T(8,128)(2,1)}, u32[]{:S(2)}) %copy-start.4) | copy-done | bytes 131096
  5.9 0.0 copy-start.5
  5.9 0.8 %copy-done.5 = bf16[2,32,1,512]{3,1,2,0:T(8,128)(2,1)S(1)} copy-done((bf16[2,32,1,512]{3,1,2,0:T(8,128)(2,1)S(1)}, bf16[2,32,1,512]{3,1,2,0:T(8,128)(2,1)}, u32[]{:S(2)}) %copy-start.5) | copy-done | bytes 65560
  6.7 0.0 copy-start.6
  6.7 0.7 %copy-done.6 = bf16[2,32,1,128]{3,1,2,0:T(8,128)(2,1)S(1)} copy-done((bf16[2,32,1,128]{3,1,2,0:T(8,128)(2,1)S(1)}, bf16[2,32,1,128]{3,1,2,0:T(8,128)(2,1)}, u32[]{:S(2)}) %copy-start.6) | copy-done | bytes 16408
  7.4 0.0 copy-start.7
  7.4 0.7 %copy-done.7 = bf16[2,32,1,128]{3,1,2,0:T(8,128)(2,1)S(1)} copy-done((bf16[2,32,1,128]{3,1,2,0:T(8,128)(2,1)S(1)}, bf16[2,32,1,128]{3,1,2,0:T(8,128)(2,1)}, u32[]{:S(2)}) %copy-start.7) | copy-done | bytes 16408
  8.1 0.0 copy-start.8
  8.1 0.7 %copy-done.8 = s32[32]{0:T(128)S(1)} copy-done((s32[32]{0:T(128)S(1)}, s32[32]{0:T(128)}, u32[]{:S(2)}) %copy-start.8) | copy-done | bytes 152
  8.8 0.0 copy-start.9
  8.8 0.7 %copy-done.9 = s32[32]{0:T(128)S(1)} copy-done((s32[32]{0:T(128)S(1)}, s32[32]{0:T(128)}, u32[]{:S(2)}) %copy-start.9) | copy-done | bytes 152
  9.4 0.0 copy-start.10
  9.4 0.7 %copy-done.10 = s32[32]{0:T(128)S(1)} copy-done((s32[32]{0:T(128)S(1)}, s32[32]{0:T(128)}, u32[]{:S(2)}) %copy-start.10) | copy-done | bytes 152
  10.1 22.6 %decode_attention.1 = bf16[64,1024]{1,0:T(8,128)(2,1)S(1)} custom-call(s32[1,32]{1,0:T(1,128)S(1)} %bitcast.23, s32[1,32]{1,0:T(1,128)S(1)} %bitcast.24, s32[1,32]{1,0:T(1,128)S(1)} %bitcast.25, bf16[64,512]{1,0:T(8,128)(2,1)S(1)} %bitcast.20, bf16[512,128]{1,0:T(8,128)(2,1)S(1)} %bitcast.17, bf16[512,128]{1,0:T(8,128)(2,1)S(1)} %bitcast.18, ...), custom_call_target="tpu_custom_call" | custom-call | tf_op jit(solution)/shard_map/decode_attention/pallas_call | solution.py:355
  32.7 0.7 %copy.13 = bf16[2,32,1024]{2,1,0:T(8,128)(2,1)} copy(bf16[2,32,1024]{2,1,0:T(8,128)(2,1)S(1)} %bitcast.15) | data formatting | bytes 262144
Async XLA Ops:
  0.0 2.2 %copy-start = (bf16[512,4096]{1,0:T(8,128)(2,1)S(1)}, bf16[512,4096]{1,0:T(8,128)(2,1)}, u32[]{:S(2)}) copy-start(bf16[512,4096]{1,0:T(8,128)(2,1)} %matrix_hbm.1) | copy-start | bytes 12582916
  2.2 0.9 %copy-start.1 = (bf16[8,16,1024]{2,1,0:T(8,128)(2,1)S(1)}, bf16[8,16,1024]{2,1,0:T(8,128)(2,1)}, u32[]{:S(2)}) copy-start(bf16[8,16,1024]{2,1,0:T(8,128)(2,1)} %param.21) | copy-start | bytes 786436
  3.1 0.9 %copy-start.2 = (bf16[32,1,16,128]{3,2,1,0:T(8,128)(2,1)S(1)}, bf16[32,1,16,128]{3,2,1,0:T(8,128)(2,1)}, u32[]{:S(2)}) copy-start(bf16[32,1,16,128]{3,2,1,0:T(8,128)(2,1)} %param.12) | copy-start | bytes 393220
  4.0 0.9 %copy-start.3 = (bf16[32,1,16,128]{3,2,1,0:T(8,128)(2,1)S(1)}, bf16[32,1,16,128]{3,2,1,0:T(8,128)(2,1)}, u32[]{:S(2)}) copy-start(bf16[32,1,16,128]{3,2,1,0:T(8,128)(2,1)} %param.13) | copy-start | bytes 393220
  4.9 0.9 %copy-start.4 = (bf16[8,1,512,16]{2,3,1,0:T(8,128)(2,1)S(1)}, bf16[8,1,512,16]{2,3,1,0:T(8,128)(2,1)}, u32[]{:S(2)}) copy-start(bf16[8,1,512,16]{2,3,1,0:T(8,128)(2,1)} %param.20) | copy-start | bytes 393220
  5.9 0.8 %copy-start.5 = (bf16[2,32,1,512]{3,1,2,0:T(8,128)(2,1)S(1)}, bf16[2,32,1,512]{3,1,2,0:T(8,128)(2,1)}, u32[]{:S(2)}) copy-start(bf16[2,32,1,512]{3,1,2,0:T(8,128)(2,1)} %param.11) | copy-start | bytes 196612
  6.7 0.7 %copy-start.6 = (bf16[2,32,1,128]{3,1,2,0:T(8,128)(2,1)S(1)}, bf16[2,32,1,128]{3,1,2,0:T(8,128)(2,1)}, u32[]{:S(2)}) copy-start(bf16[2,32,1,128]{3,1,2,0:T(8,128)(2,1)} %param.14) | copy-start | bytes 49156
  7.4 0.7 %copy-start.7 = (bf16[2,32,1,128]{3,1,2,0:T(8,128)(2,1)S(1)}, bf16[2,32,1,128]{3,1,2,0:T(8,128)(2,1)}, u32[]{:S(2)}) copy-start(bf16[2,32,1,128]{3,1,2,0:T(8,128)(2,1)} %param.15) | copy-start | bytes 49156
  8.1 0.7 %copy-start.8 = (s32[32]{0:T(128)S(1)}, s32[32]{0:T(128)}, u32[]{:S(2)}) copy-start(s32[32]{0:T(128)} %param.16) | copy-start | bytes 388
  8.8 0.7 %copy-start.9 = (s32[32]{0:T(128)S(1)}, s32[32]{0:T(128)}, u32[]{:S(2)}) copy-start(s32[32]{0:T(128)} %param.17) | copy-start | bytes 388
  9.4 0.7 %copy-start.10 = (s32[32]{0:T(128)S(1)}, s32[32]{0:T(128)}, u32[]{:S(2)}) copy-start(s32[32]{0:T(128)} %param.18) | copy-start | bytes 388

commit v2 on v1

--- a/solution.py
+++ b/solution.py
@@ -53,9 +53,9 @@
 
 def kernel(
     dims,
-    lengths_ref,
-    adapters_ref,
-    table_ref,
+    lengths_hbm,
+    adapters_hbm,
+    table_hbm,
     query_hbm,
     key_hbm,
     value_hbm,
@@ -65,6 +65,9 @@
     down_hbm,
     up_hbm,
     out_ref,
+    lengths_ref,
+    adapters_ref,
+    table_ref,
     query,
     keys,
     values,
@@ -102,11 +105,8 @@
     cached = rows * cache
     per_group = query.shape[1] // head
 
-    def ring(off):
-        return lax.rem(me + off, owners)
-
-    def back(off):
-        return lax.rem(me + owners - off, owners)
+    def other(i):
+        return lax.rem(me + 1 + i, owners)
 
     def peer(k):
         if tensors % 2:
@@ -118,7 +118,7 @@
 
     def greet(i):
         pl.semaphore_signal(
-            barrier, inc=1, device_id={"replica": ring(i + 1)}, device_id_type=MESH
+            barrier, inc=1, device_id={"replica": other(i)}, device_id_type=MESH
         )
 
     each(owners - 1, greet)
@@ -126,6 +126,9 @@
         pl.semaphore_signal(barrier, inc=1, device_id={"tensor": peer(k)}, device_id_type=MESH)
 
     loads = [
+        (adapters_hbm, adapters_ref),
+        (table_hbm, table_ref),
+        (lengths_hbm, lengths_ref),
         (query_hbm, query),
         (key_hbm, keys.at[pl.ds(0, cached)]),
         (new_key_hbm, keys.at[pl.ds(cached, steps * rows)]),
@@ -138,6 +141,9 @@
     loads = [pltpu.make_async_copy(a, b, local_sem.at[i]) for i, (a, b) in enumerate(loads)]
     for load in loads:
         load.start()
+
+    for load in loads[:2]:
+        load.wait()
 
     wanted = to_column(adapters_ref[...].astype(F32))
     total = table_ref.shape[1]
@@ -168,8 +174,6 @@
     of_local = jnp.where(of_local, 1.0, 0.0).astype(BF16)
     mask_out[...] = sum(dot(p, of_local) for p in pick).astype(BF16)
 
-    pl.semaphore_wait(barrier, owners + tensors - 2)
-
     def exchange(out, into, send, recv, dest):
         return pltpu.make_async_remote_copy(
             src_ref=out.at[aligned(dest, chunk)],
@@ -193,8 +197,8 @@
     masks = (mask_out, mask_in, mask_send, mask_recv)
     placed = (heads_out, heads_in, heads_send, heads_recv)
     deltas = (delta_out, delta_in, delta_send, delta_recv)
-    each(owners - 1, lambda i: exchange(*masks, ring(i + 1)).start())
-
+
+    loads[2].wait()
     length = to_column(lengths_ref[...].astype(F32))
     every = cached + steps * rows
     place = iota((rows, every), 1).astype(F32)
@@ -207,7 +211,7 @@
         allowed.append(jnp.where(visible, 0.0, MASKED))
     bias = jnp.concatenate(allowed, axis=0)
     scale = 1.0 / math.sqrt(head)
-    for load in loads[:5]:
+    for load in loads[3:8]:
         load.wait()
     for j in range(per_group):
         part = pl.ds(j * head, head)
@@ -222,7 +226,19 @@
     heads_out[...] = sum(
         dot(pick[s], mixed[s * rows : (s + 1) * rows]) for s in range(steps)
     ).astype(BF16)
-    each(owners - 1, lambda i: exchange(*placed, ring(i + 1)).start())
+    def base_copy(k):
+        return pltpu.make_async_remote_copy(
+            src_ref=base_out.at[k - 1],
+            dst_ref=base_in.at[k - 1],
+            send_sem=base_send.at[k - 1],
+            recv_sem=base_recv.at[k - 1],
+            device_id={"tensor": peer(k)},
+            device_id_type=MESH,
+        )
+
+    pl.semaphore_wait(barrier, owners + tensors - 2)
+    each(owners - 1, lambda i: exchange(*masks, other(i)).start())
+    each(owners - 1, lambda i: exchange(*placed, other(i)).start())
 
     def low_copy(part, k):
         return pltpu.make_async_remote_copy(
@@ -250,37 +266,27 @@
         for k in range(1, tensors):
             low_copy(part, k).start()
 
-    loads[5].wait()
+    loads[8].wait()
     own = aligned(me, chunk)
     lower(me, heads_out.at[own], mask_out.at[own])
 
-    def base_copy(k):
-        return pltpu.make_async_remote_copy(
-            src_ref=base_out.at[k - 1],
-            dst_ref=base_in.at[k - 1],
-            send_sem=base_send.at[k - 1],
-            recv_sem=base_recv.at[k - 1],
-            device_id={"tensor": peer(k)},
-            device_id_type=MESH,
-        )
-
-    loads[6].wait()
+    loads[9].wait()
     for k in range(1, tensors):
         base_out[k - 1] = dot(mixed, matrix[:, aligned(peer(k), columns)]).astype(BF16)
-        if k == 1:
-            base_copy(k).start()
     base_own[...] = dot(mixed, matrix[:, aligned(mine, columns)])
 
+    for k in range(1, tensors - 1):
+        base_copy(k).start()
+
     def lower_arrived(i):
-        source = back(i + 1)
+        source = other(i)
         here = aligned(source, chunk)
         arrival(*masks, source).wait_recv()
         arrival(*placed, source).wait_recv()
         lower(source, heads_in.at[here], mask_in.at[here])
 
     each(owners - 1, lower_arrived)
-    for k in range(2, tensors):
-        base_copy(k).start()
+    base_copy(tensors - 1).start()
 
     def raise_back(part):
         low = low_out[part].astype(F32)
@@ -289,10 +295,10 @@
             low = low + low_in[peer(k), part].astype(F32)
         return dot((ADAPTER_SCALE * low).astype(BF16), up[...]).astype(BF16)
 
-    loads[7].wait()
+    loads[10].wait()
 
     def raise_arrived(i):
-        source = back(i + 1)
+        source = other(i)
         delta_out[aligned(source, chunk)] = raise_back(source)
         exchange(*deltas, source).start()
 
@@ -303,12 +309,12 @@
         base_copy(k).wait_recv()
         base_own[...] += base_in[k - 1].astype(F32)
 
-    each(owners - 1, lambda i: arrival(*deltas, ring(i + 1)).wait_recv())
+    each(owners - 1, lambda i: arrival(*deltas, other(i)).wait_recv())
     delta = dot(unpick, delta_in[...])
     out_ref[...] = (base_own[...] + delta).astype(BF16)
 
     def sent(i):
-        dest = ring(i + 1)
+        dest = other(i)
         exchange(*masks, dest).wait_send()
         exchange(*placed, dest).wait_send()
         exchange(*deltas, dest).wait_send()
@@ -350,15 +356,18 @@
     down = jnp.swapaxes(down_maps.reshape(share, feature_width, rank), 1, 2)
     dma = pltpu.SemaphoreType.DMA
     vmem = pl.BlockSpec(memory_space=pltpu.VMEM)
-    anywhere = pl.BlockSpec(memory_space=pl.ANY)
+    hbm = pl.BlockSpec(memory_space=pltpu.HBM)
     dims = (steps, rows, cache, head, owners, tensors, share, rank, cap, chunk)
     out = pl.pallas_call(
         functools.partial(kernel, dims),
         name="decode_attention",
         out_shape=jax.ShapeDtypeStruct((steps * rows, columns), BF16),
-        in_specs=[vmem] * 3 + [anywhere] * 8,
+        in_specs=[hbm] * 11,
         out_specs=vmem,
         scratch_shapes=[
+            pltpu.VMEM((1, rows), jnp.int32),
+            pltpu.VMEM((1, rows), jnp.int32),
+            pltpu.VMEM((1, table_row_of.shape[0]), jnp.int32),
             pltpu.VMEM((steps * rows, feature_width), BF16),
             pltpu.VMEM((every, head), BF16),
             pltpu.VMEM((every, head), BF16),
@@ -377,7 +386,7 @@
             pltpu.VMEM((steps * rows, columns), F32),
             pltpu.VMEM((tensors - 1, steps * rows, columns), BF16),
             pltpu.VMEM((tensors - 1, steps * rows, columns), BF16),
-            dma((8,)),
+            dma((11,)),
             dma((owners,)),
             dma((owners,)),
             dma((owners,)),
@@ -390,7 +399,7 @@
             dma((tensors - 1,)),
         ],
         compiler_params=pltpu.CompilerParams(
-            collective_id=0, has_side_effects=True, vmem_limit_bytes=40 * 1024 * 1024
+            collective_id=0, has_side_effects=True, vmem_limit_bytes=63 * 1024 * 1024
         ),
     )(
         lengths.reshape(1, rows),

time: 33.8 us -> 24 us (0.71)
  local copies, waits for them, and re-layouts: 10.7 us -> 1.57 us
    unnamed x23 -> x1, local copies, waits for them, and re-layouts: 10.7 us -> 1.57 us
where the time goes in v2:
time: 24 us; the launch traced here: 23.8 us
  Pallas kernels  22.3 us (93%)
  local copies, waits for them, and re-layouts  1.57 us (7%)
    pallas_call x1, Pallas kernels, per_device(): pl.pallas_call(functools.partial(kernel, dims), name='decode_attention',...  22.3 us
    unnamed x1, local copies, waits for them, and re-layouts  1.57 us

profile of v2, /device:TPU:0, one launch (start us, length us, event | category | flops | bytes accessed | tf_op | source)
XLA Modules:
  0.0 23.8 jit_solution(6602036626188783205)
XLA Ops:
  0.0 22.3 %decode_attention.1 = bf16[64,1024]{1,0:T(8,128)(2,1)} custom-call(s32[1,32]{1,0:T(1,128)} %bitcast.23, s32[1,32]{1,0:T(1,128)} %bitcast.24, s32[1,32]{1,0:T(1,128)} %bitcast.25, bf16[64,512]{1,0:T(8,128)(2,1)} %bitcast.20, bf16[512,128]{1,0:T(8,128)(2,1)} %bitcast.17, bf16[512,128]{1,0:T(8,128)(2,1)} %bitcast.18, bf16[64,128]{1,0:T(8,128)(2,1)} %bitcast.21, ...), custom_call_target="tpu_custom_call" | custom-call | tf_op jit(solution)/shard_map/decode_attention/pallas_call | solution.py:361
  22.3 1.6 %copy.13 = bf16[2,32,1024]{2,1,0:T(8,128)(2,1)} copy(bf16[2,32,1024]{2,1,0:T(8,128)(2,1)} %bitcast.15) | data formatting | bytes 262144

commit v3 on v2

--- a/solution.py
+++ b/solution.py
@@ -168,11 +168,8 @@
         jnp.where(place_col == slot + s * cap, 1.0, 0.0).astype(BF16) for s in range(steps)
     ]
     unpick = jnp.concatenate(unpick, axis=0)
-    width = share * rank
-    low_column = iota((rows, width), 1).astype(F32)
-    of_local = (low_column >= local * rank) & (low_column < (local + 1.0) * rank)
-    of_local = jnp.where(of_local, 1.0, 0.0).astype(BF16)
-    mask_out[...] = sum(dot(p, of_local) for p in pick).astype(BF16)
+    taken = sum(jnp.where(place_col == slot + s * cap, local + 1.0, 0.0) for s in range(steps))
+    mask_out[0] = jnp.sum(taken, axis=0, keepdims=True) - 1.0
 
     def exchange(out, into, send, recv, dest):
         return pltpu.make_async_remote_copy(
@@ -194,7 +191,26 @@
             device_id_type=MESH,
         )
 
-    masks = (mask_out, mask_in, mask_send, mask_recv)
+    def mask_copy(dest):
+        return pltpu.make_async_remote_copy(
+            src_ref=mask_out.at[0],
+            dst_ref=mask_in.at[me],
+            send_sem=mask_send.at[dest],
+            recv_sem=mask_recv.at[me],
+            device_id={"replica": dest},
+            device_id_type=MESH,
+        )
+
+    def mask_arrival(source):
+        return pltpu.make_async_remote_copy(
+            src_ref=mask_out.at[0],
+            dst_ref=mask_in.at[source],
+            send_sem=mask_send.at[source],
+            recv_sem=mask_recv.at[source],
+            device_id={"replica": source},
+            device_id_type=MESH,
+        )
+
     placed = (heads_out, heads_in, heads_send, heads_recv)
     deltas = (delta_out, delta_in, delta_send, delta_recv)
 
@@ -237,7 +253,7 @@
         )
 
     pl.semaphore_wait(barrier, owners + tensors - 2)
-    each(owners - 1, lambda i: exchange(*masks, other(i)).start())
+    each(owners - 1, lambda i: mask_copy(other(i)).start())
     each(owners - 1, lambda i: exchange(*placed, other(i)).start())
 
     def low_copy(part, k):
@@ -260,15 +276,21 @@
             device_id_type=MESH,
         )
 
-    def lower(part, source_heads, source_mask):
-        low = dot_t(source_heads[...], down[...]) * source_mask[...].astype(F32)
+    width = share * rank
+
+    def lower(part, source_heads, locals_row):
+        here = iota((chunk, places), 1) == iota((chunk, places), 0) + me * chunk
+        first = rank * jnp.sum(jnp.where(here, locals_row, 0.0), axis=1, keepdims=True)
+        column = iota((chunk, width), 1).astype(F32)
+        of_row = (column >= first) & (column < first + rank)
+        low = jnp.where(of_row, dot_t(source_heads[...], down[...]), 0.0)
         low_out[part] = low.astype(BF16)
         for k in range(1, tensors):
             low_copy(part, k).start()
 
     loads[8].wait()
     own = aligned(me, chunk)
-    lower(me, heads_out.at[own], mask_out.at[own])
+    lower(me, heads_out.at[own], mask_out[0])
 
     loads[9].wait()
     for k in range(1, tensors):
@@ -281,9 +303,9 @@
     def lower_arrived(i):
         source = other(i)
         here = aligned(source, chunk)
-        arrival(*masks, source).wait_recv()
+        mask_arrival(source).wait_recv()
         arrival(*placed, source).wait_recv()
-        lower(source, heads_in.at[here], mask_in.at[here])
+        lower(source, heads_in.at[here], mask_in[source])
 
     each(owners - 1, lower_arrived)
     base_copy(tensors - 1).start()
@@ -315,7 +337,7 @@
 
     def sent(i):
         dest = other(i)
-        exchange(*masks, dest).wait_send()
+        mask_copy(dest).wait_send()
         exchange(*placed, dest).wait_send()
         exchange(*deltas, dest).wait_send()
 
@@ -377,8 +399,8 @@
             pltpu.VMEM((steps * rows, feature_width), BF16),
             pltpu.VMEM((places, feature_width), BF16),
             pltpu.VMEM((places, feature_width), BF16),
-            pltpu.VMEM((places, width), BF16),
-            pltpu.VMEM((places, width), BF16),
+            pltpu.VMEM((1, 1, places), F32),
+            pltpu.VMEM((owners, 1, places), F32),
             pltpu.VMEM((owners, chunk, width), BF16),
             pltpu.VMEM((tensors, owners, chunk, width), BF16),
             pltpu.VMEM((places, columns), BF16),

time: 24 us -> 23.8 us (level)
  Pallas kernels: 22.3 us -> 22 us
where the time goes in v3:
time: 23.8 us; the launch traced here: 23.6 us
  Pallas kernels  22 us (92%)
  local copies, waits for them, and re-layouts  1.57 us (7%)
    pallas_call x1, Pallas kernels, per_device(): pl.pallas_call(functools.partial(kernel, dims), name='decode_attention',...  22 us
    unnamed x1, local copies, waits for them, and re-layouts  1.57 us

profile of v3, /device:TPU:0, one launch (start us, length us, event | category | flops | bytes accessed | tf_op | source)
XLA Modules:
  0.0 23.6 jit_solution(17882599405931801513)
XLA Ops:
  0.0 22.0 %decode_attention.1 = bf16[64,1024]{1,0:T(8,128)(2,1)} custom-call(s32[1,32]{1,0:T(1,128)} %bitcast.23, s32[1,32]{1,0:T(1,128)} %bitcast.24, s32[1,32]{1,0:T(1,128)} %bitcast.25, bf16[64,512]{1,0:T(8,128)(2,1)} %bitcast.20, bf16[512,128]{1,0:T(8,128)(2,1)} %bitcast.17, bf16[512,128]{1,0:T(8,128)(2,1)} %bitcast.18, bf16[64,128]{1,0:T(8,128)(2,1)} %bitcast.21, ...), custom_call_target="tpu_custom_call" | custom-call | tf_op jit(solution)/shard_map/decode_attention/pallas_call | solution.py:383
  22.0 1.6 %copy.13 = bf16[2,32,1024]{2,1,0:T(8,128)(2,1)} copy(bf16[2,32,1024]{2,1,0:T(8,128)(2,1)} %bitcast.15) | data formatting | bytes 262144
